TPU v7x, 32 devices: a whole 2x2x4 slice. The times are simulated.
32 devices in a mesh: gx: 8 (over y, x, core), gy: 4 (over z).
Axes of the slice: x: 2, y: 2, z: 4, core: 2. Of those that a mesh axis runs over, the one named last changes fastest.
Arguments:
- field: float32 [128, 128, 1536], P('gx', 'gy'), may hold values from -24 to 24
- kappa: float32 [128, 128, 1536], P('gx', 'gy'), may hold values from 0.02 to 0.16
- history: float32 [126, 64, 32, 128], P(None, 'gx', 'gy'), may hold values from -2400 to 2400
Outputs:
- field_next: float32 [128, 128, 1536], P('gx', 'gy')
- basis: float32 [128, 64, 32, 128], P(None, 'gx', 'gy')
- factor: float32 [128, 128], replicated
All inputs are finite; a program needn't handle non-finite values.
Results may differ from a plain program's by a relative error of at most 0.00018.
Values sent between devices are 32-bit elements; how exact they have to be, the bound alone decides.
A program may use at most 192 MiB of HBM per device.

v0:
```python
import jax
import jax.numpy as jnp
from jax import lax
from jax.sharding import PartitionSpec as P


def extended(block, sides, width):
    for axis, dim in sides:
        count = lax.axis_size(axis)
        forward = [(i, i + 1) for i in range(count - 1)]
        backward = [(target, source) for source, target in forward]
        low = lax.ppermute(
            lax.slice_in_dim(block, block.shape[dim] - width, None, axis=dim), axis, forward
        )
        high = lax.ppermute(lax.slice_in_dim(block, 0, width, axis=dim), axis, backward)
        block = jnp.concatenate([low, block, high], axis=dim)
    return block


def advance(field_pad, kappa_pad):
    field_z = jnp.pad(field_pad, ((0, 0), (0, 0), (1, 1)))
    kappa_z = jnp.pad(kappa_pad, ((0, 0), (0, 0), (1, 1)))
    centre = field_z[1:-1, 1:-1, 1:-1]
    kcentre = kappa_z[1:-1, 1:-1, 1:-1]
    places = [
        (slice(2, None), slice(1, -1), slice(1, -1)),
        (slice(None, -2), slice(1, -1), slice(1, -1)),
        (slice(1, -1), slice(2, None), slice(1, -1)),
        (slice(1, -1), slice(None, -2), slice(1, -1)),
        (slice(1, -1), slice(1, -1), slice(2, None)),
        (slice(1, -1), slice(1, -1), slice(None, -2)),
    ]
    change = jnp.zeros_like(centre)
    for place in places:
        change = change + 0.5 * (kcentre + kappa_z[place]) * (field_z[place] - centre)
    return centre + change


def sample(field):
    a, b, c = field.shape
    return field.reshape(a // 2, 2, b // 4, 4, c // 12, 12)[:, 0, :, 0, :, 0]


def body(field, kappa, history):
    size_x, size_y, depth = field.shape
    both = jnp.stack([field, kappa])
    wide = extended(both, (("gx", 1), ("gy", 2)), 2)
    kappa_wide = wide[1]
    first_ext = advance(wide[0], kappa_wide)
    xpos = lax.axis_index("gx") * size_x + jnp.arange(size_x + 2, dtype=jnp.int32) - 1
    ypos = lax.axis_index("gy") * size_y + jnp.arange(size_y + 2, dtype=jnp.int32) - 1
    inside_x = (xpos >= 0) & (xpos < size_x * lax.axis_size("gx"))
    inside_y = (ypos >= 0) & (ypos < size_y * lax.axis_size("gy"))
    inside = inside_x[:, None, None] & inside_y[None, :, None]
    first_ext = jnp.where(inside, first_ext, 0.0)
    first = first_ext[1:-1, 1:-1]
    second = advance(first_ext, kappa_wide[1:-1, 1:-1])
    block = jnp.concatenate([history, sample(first)[None], sample(second)[None]], 0)
    shape = block.shape
    block = block.reshape(shape[0], -1)
    rows_all = block.shape[1] * lax.axis_size("gx") * lax.axis_size("gy")
    gram = jnp.einsum("ar,br->ab", block, block, precision=lax.Precision.HIGHEST) / rows_all
    total = lax.psum(gram, ("gx", "gy"))
    factor = jnp.linalg.cholesky(total).T
    basis = lax.linalg.triangular_solve(factor.T, block, left_side=True, lower=True)
    return (second, basis.reshape(shape), factor)


def solution(mesh):
    placed = (P("gx", "gy", None), P("gx", "gy", None), P(None, "gx", "gy", None))
    return jax.shard_map(
        body,
        mesh=mesh,
        in_specs=placed,
        out_specs=(P("gx", "gy", None), P(None, "gx", "gy", None), P()),
        check_vma=False,
    )
```

profile of v0, /device:TPU:0, one launch (start us, length us, event | category | flops | bytes accessed | tf_op | source)
XLA Modules:
  0.0 380.5 jit_solution(15627043656940403598)
XLA Ops:
  8.9 2.5 collective-permute-start
  13.3 4.7 %collective-permute-done.1 = f32[2,2,32,1536]{3,2,1,0:T(8,128)S(1)} collective-permute-done((f32[2,2,32,1536]{3,2,1,0:T(8,128)S(1)}, f32[2,2,32,1536]{3,2,1,0:T(8,128)S(1)}, u32[]{:S(2)}, u32[]{:S(2)}) %collective-permute-start.1) | collective-permute-done | bytes 786464 | tf_op jit(solution)/shard_map/ppermute | solution.py:15
  19.4 4.3 %collective-permute-start.2 = (f32[2,20,2,1536]{3,2,1,0:T(2,128)}, f32[2,20,2,1536]{3,2,1,0:T(2,128)}, u32[]{:S(2)}, u32[]{:S(2)}) collective-permute-start(f32[2,20,2,1536]{3,2,1,0:T(2,128)} %get-tuple-element.11), channel_id=1, source_target_pairs={{0,1},{1,2},{2,3},{4,5},{5,6},{6,7},{8,9},{9,10},{10,11},{12,13},{... | collective-permute-start | bytes 1474568 | tf_op jit(solution)/shard_map/ppermute | solution.py:12
  25.0 4.4 %copy.17 = f32[126,8,8,128]{3,0,2,1:T(8,128)} copy(f32[126,8,8,128]{3,2,1,0:T(8,128)S(1)} %copy-done.3) | data formatting | bytes 8257536 | tf_op args[2]
  29.3 6.0 %copy.30 = f32[126,8,8,128]{0,3,2,1:T(8,128)} copy(f32[126,8,8,128]{3,2,1,0:T(8,128)} %param.5) | data formatting | bytes 8257536 | tf_op jit(solution)/shard_map/concatenate | solution.py:58
  35.4 7.6 %pad_maximum_fusion = f32[2,20,36,1536]{3,2,1,0:T(8,128)} fusion(f32[2,20,2,1536]{3,2,1,0:T(2,128)} %collective-permute-done.3, f32[2,2,32,1536]{3,2,1,0:T(8,128)} %copy-done.6, f32[1,16,32,1536]{3,2,1,0:T(8,128)S(1)} %bitcast.34, f32[1,16,32,1536]{3,2,1,0:T(8,128)} %bitcast.36, f32[2,2,32,1536]{3,2,1,0:T(8,128)} %copy-done.5, ...), kind=kLoop, calls=%fused_computation | loop fusion | flops 11059200 | bytes 17694720 | tf_op jit(solution)/shard_map/concatenate | solution.py:16
  43.0 7.1 %slice_bitcast_fusion.1 = (f32[20,36,1536]{2,1,0:T(8,128)}, f32[20,36,1536]{2,1,0:T(8,128)S(1)}) fusion(f32[2,20,36,1536]{3,2,1,0:T(8,128)} %pad_maximum_fusion), kind=kLoop, calls=%fused_computation.6 | loop fusion | bytes 17694720 | tf_op jit(solution)/shard_map/squeeze | solution.py:49
  50.1 24.4 %fusion.6 = (f32[18,34,1536]{2,1,0:T(8,128)}, f32[18,34,1536]{2,1,0:T(8,128)}) fusion(f32[20,36,1536]{2,1,0:T(8,128)S(1)} %get-tuple-element.10, f32[20,36,1536]{2,1,0:T(8,128)} %get-tuple-element.9, pred[18,34]{1,0:T(8,128)(4,1)S(1)} %broadcast_and_fusion), kind=kLoop, calls=%fused_computation.17 | loop fusion | flops 29140992 | bytes 61590528 | tf_op jit(solution)/shard_map/jit(_where)/select_n | solution.py:55
  74.4 29.3 %fusion.62 = (f32[16,32,1536]{2,1,0:T(8,128)}, f32[16,32,1536]{2,1,0:T(8,128)S(1)}) fusion(f32[18,34,1536]{2,1,0:T(8,128)} %get-tuple-element.15, f32[18,34,1536]{2,1,0:T(8,128)} %get-tuple-element.16, f32[20,36,1536]{2,1,0:T(8,128)} %copy-done), kind=kLoop, calls=%fused_computation.102 | loop fusion | flops 23592960 | bytes 46596096 | tf_op jit(solution)/shard_map/slice | solution.py:23
  103.8 39.5 %reshape.77 = f32[8,2,8,4,128,12]{5,4,3,2,1,0:T(8,128)} reshape(f32[16,32,1536]{2,1,0:T(8,128)} %get-tuple-element.17) | data formatting | bytes 6291456 | tf_op jit(solution)/shard_map/reshape | solution.py:41
  143.3 4.7 %slice.203 = f32[8,1,8,1,128,1]{5,4,3,2,1,0:T(8,128)} slice(f32[8,2,8,4,128,12]{5,4,3,2,1,0:T(8,128)} %reshape.77), slice={[0:8], [0:1], [0:8], [0:1], [0:128], [0:1]} | slice | bytes 65536 | tf_op jit(solution)/shard_map/slice | solution.py:41
  148.0 2.8 copy.31
  150.8 38.2 %reshape.78 = f32[8,2,8,4,128,12]{5,4,3,2,1,0:T(8,128)} reshape(f32[16,32,1536]{2,1,0:T(8,128)S(1)} %get-tuple-element.18) | data formatting | bytes 6291456 | tf_op jit(solution)/shard_map/reshape | solution.py:41
  189.0 4.7 %slice.204 = f32[8,1,8,1,128,1]{5,4,3,2,1,0:T(8,128)} slice(f32[8,2,8,4,128,12]{5,4,3,2,1,0:T(8,128)} %reshape.78), slice={[0:8], [0:1], [0:8], [0:1], [0:128], [0:1]} | slice | bytes 65536 | tf_op jit(solution)/shard_map/slice | solution.py:41
  193.7 2.8 copy.32
  196.5 7.7 %fusion.54 = f32[128,128]{0,1:T(8,128)} fusion(f32[1,8,8,128]{3,0,2,1:T(1,128)S(1)} %bitcast.42, f32[1,8,8,128]{3,0,2,1:T(1,128)S(1)} %bitcast.40, f32[126,8,8,128]{3,0,2,1:T(8,128)} %copy.17), kind=kOutput, calls=%fused_computation.82 | convolution fusion | flops 1612726272 | bytes 4259840 | tf_op jit(solution)/shard_map/ar,br->ab/dot_general | solution.py:62
  204.3 2.7 copy.21
  207.0 2.8 copy.22
  209.8 8.8 %pad_maximum_fusion.1 = f32[128,8192]{0,1:T(8,128)} fusion(f32[1,8192]{0,1:T(8,128)} %copy.22, f32[1,8192]{0,1:T(8,128)} %copy.21, f32[126,8192]{0,1:T(8,128)} %bitcast.38), kind=kLoop, calls=%fused_computation.48 | loop fusion | flops 2097152 | bytes 8388608 | tf_op jit(solution)/shard_map/concatenate | solution.py:58
  218.6 119.2 %all-reduce.6.cloned.1.call-done = f32[128,128]{0,1:T(8,128)} async-done(((f32[128,128]{0,1:T(8,128)}), f32[128,128]{0,1:T(8,128)}) %all-reduce.6.cloned.1.call-update) | async-done | bytes 65552 | tf_op jit(solution)/shard_map/psum | solution.py:63
  339.6 11.7 %cholesky.16 = f32[128,128]{1,0:T(8,128)S(1)} custom-call(f32[128,128]{1,0:T(8,128)S(1)} %fusion.59), custom_call_target="Cholesky" | custom-call | tf_op jit(solution)/shard_map/jit(cholesky)/cholesky | solution.py:64
  352.7 9.8 %custom-call.6 = f32[1,128,128]{1,2,0:T(8,128)S(1)} custom-call(f32[1,128,128]{2,1,0:T(8,128)S(1)} %get-tuple-element.20), custom_call_target="InvertDiagBlocksLowerTriangular" | custom-call | tf_op jit(solution)/shard_map/triangular_solve | solution.py:65
  362.5 5.7 %fusion.57 = f32[128,8,8,128]{3,0,2,1:T(8,128)S(1)} fusion(f32[8,8,128,128]{3,2,1,0:T(8,128)} %bitcast.39, f32[1,128,128]{1,2,0:T(8,128)S(1)} %custom-call.6), kind=kOutput, calls=%fused_computation.87 | convolution fusion | flops 1610612736 | bytes 8454144 | tf_op jit(solution)/shard_map/triangular_solve | solution.py:65
  368.2 4.4 %copy.24 = f32[128,8,8,128]{3,2,1,0:T(8,128)} copy(f32[128,8,8,128]{3,0,2,1:T(8,128)S(1)} %fusion.57) | data formatting | bytes 8388608
  (32 shorter events, 10.2 us)
Async XLA Ops:
  7.2 10.8 %copy-start.1 = (f32[16,32,1536]{2,1,0:T(8,128)S(1)}, f32[16,32,1536]{2,1,0:T(8,128)}, u32[]{:S(2)}) copy-start(f32[16,32,1536]{2,1,0:T(8,128)} %param.4) | copy-start | bytes 9437188
  7.2 330.7 %all-reduce.6.cloned.1.call-start = ((), (), s32[]{:S(2)}) async-start(), calls=%async_computation | async-start | bytes 131072 | tf_op jit(solution)/shard_map/psum | solution.py:63
  7.2 10.7 %copy-start.2 = (f32[16,32,1536]{2,1,0:T(8,128)S(1)}, f32[16,32,1536]{2,1,0:T(8,128)}, u32[]{:S(2)}) copy-start(f32[16,32,1536]{2,1,0:T(8,128)} %param.3) | copy-start | bytes 9437188
  8.9 4.4 %collective-permute-start = (f32[2,2,32,1536]{3,2,1,0:T(8,128)S(1)}, f32[2,2,32,1536]{3,2,1,0:T(8,128)S(1)}, u32[]{:S(2)}, u32[]{:S(2)}) collective-permute-start(f32[2,2,32,1536]{3,2,1,0:T(8,128)S(1)} %get-tuple-element.13), channel_id=1, source_target_pairs={{0,4},{4,8},{8,12},{12,16},{16,20},{20,24},{24,28},{1,5},{5,9},{9,... | collective-permute-start | bytes 2359304 | tf_op jit(solution)/shard_map/ppermute | solution.py:12
  11.4 13.5 %copy-start.3 = (f32[126,8,8,128]{3,2,1,0:T(8,128)S(1)}, f32[126,8,8,128]{3,2,1,0:T(8,128)}, u32[]{:S(2)}) copy-start(f32[126,8,8,128]{3,2,1,0:T(8,128)} %param.5) | copy-start | bytes 12386308
  11.5 6.5 %collective-permute-start.1 = (f32[2,2,32,1536]{3,2,1,0:T(8,128)S(1)}, f32[2,2,32,1536]{3,2,1,0:T(8,128)S(1)}, u32[]{:S(2)}, u32[]{:S(2)}) collective-permute-start(f32[2,2,32,1536]{3,2,1,0:T(8,128)S(1)} %get-tuple-element.14), channel_id=1, source_target_pairs={{4,0},{8,4},{12,8},{16,12},{20,16},{24,20},{28,24},{5,1},{9,5},{13... | collective-permute-start | bytes 2359304 | tf_op jit(solution)/shard_map/ppermute | solution.py:15
  13.3 6.1 %copy-start.5 = (f32[2,2,32,1536]{3,2,1,0:T(8,128)}, f32[2,2,32,1536]{3,2,1,0:T(8,128)S(1)}, u32[]{:S(2)}) copy-start(f32[2,2,32,1536]{3,2,1,0:T(8,128)S(1)} %collective-permute-done) | copy-start | bytes 2359300
  18.0 1.4 copy-start.6
  19.4 16.0 %collective-permute-start.2 = (f32[2,20,2,1536]{3,2,1,0:T(2,128)}, f32[2,20,2,1536]{3,2,1,0:T(2,128)}, u32[]{:S(2)}, u32[]{:S(2)}) collective-permute-start(f32[2,20,2,1536]{3,2,1,0:T(2,128)} %get-tuple-element.11), channel_id=1, source_target_pairs={{0,1},{1,2},{2,3},{4,5},{5,6},{6,7},{8,9},{9,10},{10,11},{12,13},{... | collective-permute-start | bytes 1474568 | tf_op jit(solution)/shard_map/ppermute | solution.py:12
  23.7 11.7 %collective-permute-start.3 = (f32[2,20,2,1536]{3,2,1,0:T(2,128)}, f32[2,20,2,1536]{3,2,1,0:T(2,128)}, u32[]{:S(2)}, u32[]{:S(2)}) collective-permute-start(f32[2,20,2,1536]{3,2,1,0:T(2,128)} %get-tuple-element.12), channel_id=1, source_target_pairs={{1,0},{2,1},{3,2},{5,4},{6,5},{7,6},{9,8},{10,9},{11,10},{13,12},{... | collective-permute-start | bytes 1474568 | tf_op jit(solution)/shard_map/ppermute | solution.py:15
  50.1 24.4 %copy-start = (f32[20,36,1536]{2,1,0:T(8,128)}, f32[20,36,1536]{2,1,0:T(8,128)S(1)}, u32[]{:S(2)}) copy-start(f32[20,36,1536]{2,1,0:T(8,128)S(1)} %get-tuple-element.10) | copy-start | bytes 13271044
  103.8 47.1 %copy-start.4 = (f32[16,32,1536]{2,1,0:T(8,128)}, f32[16,32,1536]{2,1,0:T(8,128)S(1)}, u32[]{:S(2)}) copy-start(f32[16,32,1536]{2,1,0:T(8,128)S(1)} %get-tuple-element.18) | copy-start | bytes 9437188
Sparse Core Ops, SparseCore 0:
  204.4 133.3 all-reduce.5
where the time goes:
time: 386 us; the launch traced here: 381 us
  waiting for transfers between devices  124 us (32%)
  local copies, waits for them, and re-layouts  122 us (32%)
  other arithmetic  97 us (25%)
  between operations  14.4 us (4%)
  matrix products  13.4 us (3%)
  starting transfers between devices  9.71 us (3%)
    psum x1, waiting for transfers between devices, body(): total = lax.psum(gram, ('gx', 'gy'))  119 us
    reshape x2, local copies, waits for them, and re-layouts, sample(): return field.reshape(a // 2, 2, b // 4, 4, c // 12, 12)[:, 0, :, 0, :, 0]  77.7 us
    slice x1, other arithmetic, advance(): centre = field_z[1:-1, 1:-1, 1:-1]  29.3 us
    select_n x1, other arithmetic, body(): first_ext = jnp.where(inside, first_ext, 0.0)  24.4 us
    unnamed x19, local copies, waits for them, and re-layouts  15.2 us
    another operation x3, other arithmetic, body(): factor = jnp.linalg.cholesky(total).T  12.4 us
    concatenate x3, local copies, waits for them, and re-layouts, body(): jnp.concatenate([history, sample(first)[None], sample(second)[None]], 0)  11.5 us
    another operation x1, other arithmetic, body(): lax.linalg.triangular_solve(factor.T, block, left_side=True, lower=True)  9.81 us
  transfers between devices with their start and end apart: 5, of which 3 were waited for; matrix products, arithmetic and copies ran while one was open for 7% of the time, Pallas kernels for 0%

commit v1 on v0

v1 whole, which is shorter than its diff:
```python
import functools

import jax
import jax.numpy as jnp
from jax import lax
from jax.experimental import pallas as pl
from jax.experimental.pallas import tpu as pltpu
from jax.sharding import PartitionSpec as P

F32 = jnp.float32
BF16 = jnp.bfloat16
TOP = 8
MESH = pl.DeviceIdType.MESH


def dot(a, b, contract):
    return lax.dot_general(
        a, b, ((contract[:1], contract[1:]), ((), ())), preferred_element_type=F32
    )


def split(x):
    hi = x.astype(BF16)
    return hi, (x - hi.astype(F32)).astype(BF16)


def stencil(v, k, out, tiles):
    size_x = v.shape[0] - 2
    depth = v.shape[2]
    lane = lax.broadcasted_iota(jnp.int32, (8, depth), 1)

    for tile in tiles:
        at = TOP + 8 * tile
        rows = pl.ds(at, 8)
        up = pl.ds(at + 1, 8)
        down = pl.ds(at - 1, 8)

        def layer(x, flux):
            c, kc = v[x, rows, :], k[x, rows, :]
            ahead = (kc + k[x + 1, rows, :]) * (v[x + 1, rows, :] - c)
            acc = ahead - flux
            acc += (kc + k[x, up, :]) * (v[x, up, :] - c)
            acc += (kc + k[x, down, :]) * (v[x, down, :] - c)
            last = lane == depth - 1
            c_up = jnp.where(last, 0.0, pltpu.roll(c, depth - 1, 1))
            k_up = jnp.where(last, 0.0, pltpu.roll(kc, depth - 1, 1))
            face = (kc + k_up) * (c_up - c)
            acc += face
            acc -= jnp.where(lane == 0, kc * c, pltpu.roll(face, 1, 1))
            out[x, rows, :] = c + 0.5 * acc
            return ahead

        first = (k[0, rows, :] + k[1, rows, :]) * (v[1, rows, :] - v[0, rows, :])
        lax.fori_loop(1, size_x + 1, layer, first)


def sample(v, pick, rows_y):
    parts = []
    for x in range(1, v.shape[0] - 1, 2):
        parts += [v[x, pl.ds(TOP + 4 * y, 1), :] for y in range(rows_y)]
    x = jnp.concatenate(parts, axis=0)
    hi = x.astype(BF16)
    rest = x - hi.astype(F32)
    mid = rest.astype(BF16)
    low = (rest - mid.astype(F32)).astype(BF16)
    n = x.shape[0]
    got = dot(jnp.concatenate([hi, mid, low], axis=0), pick, (1, 0))
    return got[:n] + got[n : 2 * n] + got[2 * n :]


def evolve(
    nx, ny, past, field, kappa, hist, second_o, s_o, gram_o,
    f, k, v, block, s, gram, slots, red, total, load, halo_send, halo_recv, rs_send, rs_recv, ag_send, ag_recv,
):
    size_x, size_y, depth = field.shape
    gx, gy = lax.axis_index("gx"), lax.axis_index("gy")
    devices = nx * ny
    snaps = gram.shape[0]
    owners = snaps // 8
    step = devices // owners
    me = gy * nx + gx

    def device(flat):
        return (lax.rem(flat, nx), lax.div(flat, nx))

    barrier = pltpu.get_barrier_semaphore()

    def greet(i, carry):
        pl.semaphore_signal(barrier, inc=1, device_id=device(lax.rem(me + i, devices)), device_id_type=MESH)
        return carry

    lax.fori_loop(1, devices, greet, 0)

    inner = (pl.ds(1, size_x), pl.ds(TOP, size_y))
    loads = [
        pltpu.make_async_copy(field, f.at[inner], load.at[0]),
        pltpu.make_async_copy(kappa, k.at[inner], load.at[1]),
        pltpu.make_async_copy(hist, block.at[pl.ds(0, hist.shape[0])], load.at[2]),
    ]
    for copy in loads:
        copy.start()

    left, right = gx > 0, gx < nx - 1
    below, above = gy > 0, gy < ny - 1
    whole_y = pl.ds(TOP, size_y)
    whole_x = pl.ds(1, size_x)
    sides = [
        (left, right, (gx - 1, gy), (1, whole_y), (size_x + 1, whole_y)),
        (right, left, (gx + 1, gy), (size_x, whole_y), (0, whole_y)),
        (below, above, (gx, gy - 1), (whole_x, pl.ds(TOP, 1)), (whole_x, pl.ds(TOP + size_y, 1))),
        (above, below, (gx, gy + 1), (whole_x, pl.ds(TOP + size_y - 1, 1)), (whole_x, pl.ds(TOP - 1, 1))),
    ]

    def halo(ref, which, side):
        to, _, place, src, dst = sides[side]
        return pltpu.make_async_remote_copy(
            src_ref=ref.at[src], dst_ref=ref.at[dst],
            send_sem=halo_send.at[which, side], recv_sem=halo_recv.at[which, side],
            device_id=place, device_id_type=MESH,
        )

    def exchange(ref, which, order):
        for side in order:
            pl.when(sides[side][0])(halo(ref, which, side).start)

    def arrive(ref, which):
        for side in range(4):
            pl.when(sides[side][1])(halo(ref, which, side).wait_recv)

    def sent(ref, which):
        for side in range(4):
            pl.when(sides[side][0])(halo(ref, which, side).wait_send)

    for ref in (f, k, v):
        for side in range(4):
            dst = sides[side][4]

            @pl.when(jnp.logical_not(sides[side][1]))
            def _(ref=ref, dst=dst, side=side):
                if side < 2:
                    ref[dst[0], dst[1], :] = jnp.zeros((size_y, depth), F32)
                else:
                    for x in range(size_x):
                        ref[x + 1, dst[1], :] = jnp.zeros((1, depth), F32)

    pl.semaphore_wait(barrier, devices - 1)
    loads[0].wait()
    exchange(f, 0, range(4))
    loads[1].wait()
    exchange(k, 1, range(4))

    samples = depth // 12
    pick = (
        lax.broadcasted_iota(jnp.int32, (depth, samples), 0)
        == 12 * lax.broadcasted_iota(jnp.int32, (depth, samples), 1)
    ).astype(F32).astype(BF16)

    arrive(f, 0)
    arrive(k, 1)
    tiles = size_y // 8
    edge = sorted({0, tiles - 1})
    middle = [t for t in range(tiles) if t not in edge]
    stencil(f, k, v, edge)
    exchange(v, 2, (2, 3))
    stencil(f, k, v, middle)
    exchange(v, 2, (0, 1))

    loads[2].wait()
    cells = hist.shape[0] // past
    block[pl.ds(past * cells, cells), :] = sample(v, pick, size_y // 4)
    sent(f, 0)
    sent(k, 1)
    arrive(v, 2)
    stencil(v, k, f, range(tiles))
    out = pltpu.make_async_copy(f.at[inner], second_o, load.at[0])
    out.start()
    block[pl.ds((past + 1) * cells, cells), :] = sample(f, pick, size_y // 4)
    sent(v, 2)

    def pair(p, acc):
        x = jnp.concatenate(
            [block[pl.ds(2 * p, snaps, stride=cells), :], block[pl.ds(2 * p + 1, snaps, stride=cells), :]], axis=1
        )
        both = jnp.concatenate(split(x), axis=0)
        s[p] = both
        return acc + dot(both, both, (1, 1))

    acc = lax.fori_loop(0, cells // 2, pair, jnp.zeros((2 * snaps, 2 * snaps), F32))
    gram[...] = (acc[:snaps, :snaps] + acc[snaps:, snaps:]) + (acc[:snaps, snaps:] + acc[snaps:, :snaps])
    keep = pltpu.make_async_copy(s, s_o, load.at[1])
    keep.start()

    is_owner = lax.rem(me, step) == 0
    mine = lax.div(me, step)

    def scatter(j):
        return pltpu.make_async_remote_copy(
            src_ref=gram.at[pl.ds(8 * j, 8)], dst_ref=slots.at[me],
            send_sem=rs_send.at[j], recv_sem=rs_recv.at[me],
            device_id=device(j * step), device_id_type=MESH,
        )

    def start_scatter(j, carry):
        pl.when(j * step != me)(lambda: scatter(j).start())
        return carry

    def end_scatter(j, carry):
        pl.when(j * step != me)(lambda: scatter(j).wait_send())
        return carry

    lax.fori_loop(0, owners, start_scatter, 0)

    def gather(i):
        to = lax.rem(me + i, devices)
        return pltpu.make_async_remote_copy(
            src_ref=red, dst_ref=total.at[pl.ds(8 * mine, 8)],
            send_sem=ag_send.at[i], recv_sem=ag_recv.at[mine],
            device_id=device(to), device_id_type=MESH,
        )


    @pl.when(is_owner)
    def _():
        own = pl.ds(pl.multiple_of(8 * mine, 8), 8)
        slots[me] = gram[own, :]

        def take(i, carry):
            source = lax.rem(me + i, devices)
            pltpu.make_async_remote_copy(
                src_ref=gram.at[pl.ds(0, 8)], dst_ref=slots.at[source],
                send_sem=rs_send.at[0], recv_sem=rs_recv.at[source],
                device_id=device(source), device_id_type=MESH,
            ).wait_recv()
            return carry

        lax.fori_loop(1, devices, take, 0)
        red[...] = jnp.sum(slots[...], axis=0) * (1.0 / (cells * samples * devices))
        total[own, :] = red[...]

        def give(i, carry):
            gather(i).start()
            return carry

        lax.fori_loop(1, devices, give, 0)

        def given(i, carry):
            gather(i).wait_send()
            return carry

        lax.fori_loop(1, devices, given, 0)

    def get(j, carry):
        @pl.when(j * step != me)
        def _():
            pltpu.make_async_remote_copy(
                src_ref=red, dst_ref=total.at[pl.ds(8 * j, 8)],
                send_sem=ag_send.at[0], recv_sem=ag_recv.at[j],
                device_id=device(j * step), device_id_type=MESH,
            ).wait_recv()

        return carry

    lax.fori_loop(0, owners, get, 0)
    lax.fori_loop(0, owners, end_scatter, 0)
    gram_o[...] = total[...]
    out.wait()
    keep.wait()


def eliminate(gram, width=4):
    n = gram.shape[0]
    row = lax.broadcasted_iota(jnp.int32, (n, n), 0)
    col = lax.broadcasted_iota(jnp.int32, (n, n), 1)
    a, w = gram, (row == col).astype(F32)
    for k in range(0, n, width):
        cols, rows_a, rows_w = [], [], []
        low = k // 8 * 8
        for j in range(k, k + width):
            c = jnp.broadcast_to(a[low:, j : j + 1], (n - low, n))
            ra, rw = a[j : j + 1, :], w[j : j + 1, :]
            for i in range(len(cols)):
                factor = cols[i][j - low : j - low + 1, :]
                c = c - cols[i] * factor
                ra = ra - rows_a[i] * factor
                rw = rw - rows_w[i] * factor
            scale = lax.rsqrt(c[j - low : j - low + 1, :])
            cols.append(c * scale)
            rows_a.append(ra * scale)
            rows_w.append(rw * scale)
        below = row[low:] >= k + width
        ta, tw = a[low:], w[low:]
        for j in range(width):
            c = jnp.where(below, cols[j], 0.0)
            here = row[low:] == k + j
            ta = jnp.where(here, rows_a[j], ta - c * rows_a[j])
            tw = jnp.where(here, rows_w[j], tw - c * rows_w[j])
        a = ta if low == 0 else jnp.concatenate([a[:low], ta], axis=0)
        w = tw if low == 0 else jnp.concatenate([w[:low], tw], axis=0)
    return jnp.where(col >= row, a, 0.0), jnp.where(col <= row, w, 0.0)


def orthogonalize(gram, s, second, factor_o, basis_o, next_o, s_v, out, sem, out_sem):
    snaps = gram.shape[0]
    keep = pltpu.make_async_copy(second, next_o, sem.at[0])
    keep.start()
    get = pltpu.make_async_copy(s, s_v, sem.at[1])
    get.start()
    factor, inverse = eliminate(gram[...])
    factor_o[...] = factor
    hi, low = split(inverse)
    both = jnp.concatenate([jnp.concatenate([hi, hi], axis=1), jnp.concatenate([low, low], axis=1)], axis=0)
    get.wait()
    per_x = basis_o.shape[2]

    def layer(x):
        return pltpu.make_async_copy(out.at[x], basis_o.at[:, x], out_sem.at[x])

    def body(x, carry):
        target = out.at[x].reshape(snaps * per_x, out.shape[3])
        for p in range(per_x // 2):
            got = dot(both, s_v[x * (per_x // 2) + p], (1, 0))
            got = got[:snaps] + got[snaps:]
            n = got.shape[1] // 2
            target[pl.ds(2 * p, snaps, stride=per_x), :] = got[:, :n]
            target[pl.ds(2 * p + 1, snaps, stride=per_x), :] = got[:, n:]
        layer(x).start()
        return carry

    lax.fori_loop(0, out.shape[0], body, 0)
    for x in range(out.shape[0]):
        layer(x).wait()
    keep.wait()


def body(nx, ny, field, kappa, history):
    size_x, size_y, depth = field.shape
    past, cells_x, cells_y, samples = history.shape
    cells = cells_x * cells_y
    snaps = past + 2
    owners = snaps // 8
    devices = nx * ny
    anywhere = pl.BlockSpec(memory_space=pl.ANY)
    vmem = pl.BlockSpec(memory_space=pltpu.VMEM)
    padded = pltpu.VMEM((size_x + 2, size_y + 2 * TOP, depth), F32)
    stacked = (cells // 2, 2 * snaps, 2 * samples)
    dma = pltpu.SemaphoreType.DMA
    second, s, gram = pl.pallas_call(
        functools.partial(evolve, nx, ny, past),
        out_shape=[
            jax.ShapeDtypeStruct(field.shape, F32),
            jax.ShapeDtypeStruct(stacked, BF16),
            jax.ShapeDtypeStruct((snaps, snaps), F32),
        ],
        in_specs=[anywhere] * 3,
        out_specs=[anywhere, anywhere, vmem],
        scratch_shapes=[
            padded, padded, padded,
            pltpu.VMEM((snaps * cells, samples), F32),
            pltpu.VMEM(stacked, BF16),
            pltpu.VMEM((snaps, snaps), F32),
            pltpu.VMEM((devices, 8, snaps), F32),
            pltpu.VMEM((8, snaps), F32),
            pltpu.VMEM((snaps, snaps), F32),
            dma((3,)), dma((3, 4)), dma((3, 4)),
            dma((owners,)), dma((devices,)), dma((devices,)), dma((owners,)),
        ],
        compiler_params=pltpu.CompilerParams(
            collective_id=0, has_side_effects=True, vmem_limit_bytes=48 << 20
        ),
        name="evolve",
    )(field, kappa, history.reshape(past * cells, samples))
    factor, basis, field_next = pl.pallas_call(
        orthogonalize,
        out_shape=[
            jax.ShapeDtypeStruct((snaps, snaps), F32),
            jax.ShapeDtypeStruct((snaps, cells_x, cells_y, samples), F32),
            jax.ShapeDtypeStruct(field.shape, F32),
        ],
        in_specs=[vmem, anywhere, anywhere],
        out_specs=[vmem, anywhere, anywhere],
        scratch_shapes=[
            pltpu.VMEM(stacked, BF16),
            pltpu.VMEM((cells_x, snaps, cells_y, samples), F32),
            dma((2,)), dma((cells_x,)),
        ],
        compiler_params=pltpu.CompilerParams(vmem_limit_bytes=48 << 20),
        name="orthogonalize",
    )(gram, s, second)
    return field_next, basis, factor


def solution(mesh):
    placed = (P("gx", "gy", None), P("gx", "gy", None), P(None, "gx", "gy", None))
    return jax.shard_map(
        functools.partial(body, mesh.shape["gx"], mesh.shape["gy"]),
        mesh=mesh,
        in_specs=placed,
        out_specs=(P("gx", "gy", None), P(None, "gx", "gy", None), P()),
        check_vma=False,
    )
```

time: 386 us -> 73.5 us (0.19); the launches traced: 381 us -> 73.4 us
  waiting for transfers between devices: 124 us -> 0 us
  local copies, waits for them, and re-layouts: 122 us -> 0 us
  other arithmetic: 97 us -> 0 us
  Pallas kernels: 0 us -> 72.8 us
  between operations: 14.4 us -> 0.64 us
  matrix products: 13.4 us -> 0 us
  starting transfers between devices: 9.71 us -> 0 us
    psum x1 -> x0, waiting for transfers between devices: 119 us -> none  [body(): total = lax.psum(gram, ('gx', 'gy'))]
    reshape x2 -> x0, local copies, waits for them, and re-layouts: 77.7 us -> none  [sample(): return field.reshape(a // 2, 2, b // 4, 4, c // 12, 12)[:, 0, :, 0, :, 0]]
    pallas_call x0 -> x2, Pallas kernels: none -> 72.8 us  [the longest x1 64.2 us: body(): pl.pallas_call(functools.partial(evolve, nx, ny, past), out_shape=[jax.Sh...]
    slice x3 -> x0, other arithmetic: 32.4 us -> none  [the longest x1 29.3 us: advance(): centre = field_z[1:-1, 1:-1, 1:-1]]
    select_n x1 -> x0, other arithmetic: 24.4 us -> none  [body(): first_ext = jnp.where(inside, first_ext, 0.0)]
    another operation x4 -> x0, other arithmetic: 22.2 us -> none  [the longest x3 12.4 us: body(): factor = jnp.linalg.cholesky(total).T]
    concatenate x2 -> x0, other arithmetic: 16.5 us -> none  [the longest x1 8.84 us: body(): jnp.concatenate([history, sample(first)[None], sample(second)[None]], 0)]
    unnamed x19 -> x0, local copies, waits for them, and re-layouts: 15.2 us -> none
  transfers between devices with their start and end apart: 5 -> 0, of which waited for: 3 -> 0; matrix products, arithmetic and copies ran while one was open for 7% -> 0% of each run, Pallas kernels for 0% -> 0%
where the time goes in v1:
time: 73.5 us; the launch traced here: 73.4 us
  Pallas kernels  72.8 us (99%)
    pallas_call x1, Pallas kernels, body(): pl.pallas_call(functools.partial(evolve, nx, ny, past), out_shape=[jax.Sh...  64.2 us
    pallas_call x1, Pallas kernels, body(): pl.pallas_call(orthogonalize, out_shape=[jax.ShapeDtypeStruct((snaps, sna...  8.57 us

profile of v1, /device:TPU:0, one launch (start us, length us, event | category | flops | bytes accessed | tf_op | source)
XLA Modules:
  0.0 73.4 jit_solution(17110765571124032547)
XLA Ops:
  0.6 64.2 %evolve.1 = (f32[16,32,1536]{2,1,0:T(8,128)S(1)}, bf16[32,256,256]{2,1,0:T(8,128)(2,1)}, f32[128,128]{1,0:T(8,128)S(1)}) custom-call(f32[16,32,1536]{2,1,0:T(8,128)} %field.1, f32[16,32,1536]{2,1,0:T(8,128)} %kappa.1, f32[8064,128]{1,0:T(8,128)} %bitcast.1), custom_call_target="tpu_custom_call" | custom-call | tf_op jit(solution)/shard_map/evolve/pallas_call | solution.py:347
  64.8 8.6 %orthogonalize.1 = (f32[128,128]{1,0:T(8,128)}, f32[128,8,8,128]{3,2,1,0:T(8,128)}, f32[16,32,1536]{2,1,0:T(8,128)}) custom-call(f32[128,128]{1,0:T(8,128)S(1)} %get-tuple-element.9.gram, bf16[32,256,256]{2,1,0:T(8,128)(2,1)} %get-tuple-element.10.s, f32[16,32,1536]{2,1,0:T(8,128)S(1)} %get-tuple-element.11.second), custom_call_target="tpu_custom_call" | custom-call | tf_op jit(solution)/shard_map/orthogonalize/pallas_call | solution.py:372

commit v2 on v1

--- a/solution.py
+++ b/solution.py
@@ -44,14 +44,15 @@
             last = lane == depth - 1
             c_up = jnp.where(last, 0.0, pltpu.roll(c, depth - 1, 1))
             k_up = jnp.where(last, 0.0, pltpu.roll(kc, depth - 1, 1))
-            face = (kc + k_up) * (c_up - c)
-            acc += face
-            acc -= jnp.where(lane == 0, kc * c, pltpu.roll(face, 1, 1))
+            acc += (kc + k_up) * (c_up - c)
+            c_down = jnp.where(lane == 0, 0.0, pltpu.roll(c, 1, 1))
+            k_down = jnp.where(lane == 0, 0.0, pltpu.roll(kc, 1, 1))
+            acc += (kc + k_down) * (c_down - c)
             out[x, rows, :] = c + 0.5 * acc
             return ahead
 
         first = (k[0, rows, :] + k[1, rows, :]) * (v[1, rows, :] - v[0, rows, :])
-        lax.fori_loop(1, size_x + 1, layer, first)
+        lax.fori_loop(1, size_x + 1, layer, first, unroll=4)
 
 
 def sample(v, pick, rows_y):
@@ -70,7 +71,8 @@
 
 def evolve(
     nx, ny, past, field, kappa, hist, second_o, s_o, gram_o,
-    f, k, v, block, s, gram, slots, red, total, load, halo_send, halo_recv, rs_send, rs_recv, ag_send, ag_recv,
+    f, k, v, block, s, gram, slots, red, total, ends,
+    load, halo_send, halo_recv, rs_send, rs_recv, ag_send, ag_recv, end_send, end_recv,
 ):
     size_x, size_y, depth = field.shape
     gx, gy = lax.axis_index("gx"), lax.axis_index("gy")
@@ -155,6 +157,50 @@
         == 12 * lax.broadcasted_iota(jnp.int32, (depth, samples), 1)
     ).astype(F32).astype(BF16)
 
+    loads[2].wait()
+    cells = hist.shape[0] // past
+    block[pl.ds(past * cells, 2 * cells), :] = jnp.zeros((2 * cells, samples), F32)
+
+    def pair(p, acc):
+        x = jnp.concatenate(
+            [block[pl.ds(2 * p, snaps, stride=cells), :], block[pl.ds(2 * p + 1, snaps, stride=cells), :]], axis=1
+        )
+        both = jnp.concatenate(split(x), axis=0)
+        s[p] = both
+        return acc + dot(both, both, (1, 1))
+
+    acc = lax.fori_loop(0, cells // 2, pair, jnp.zeros((2 * snaps, 2 * snaps), F32), unroll=2)
+    gram[...] = (acc[:snaps, :snaps] + acc[snaps:, snaps:]) + (acc[:snaps, snaps:] + acc[snaps:, :snaps])
+
+    is_owner = (lax.rem(me, step) == 0) & (me < (owners - 1) * step)
+    mine = lax.div(me, step)
+
+    def scatter(j):
+        return pltpu.make_async_remote_copy(
+            src_ref=gram.at[pl.ds(8 * j, 8)], dst_ref=slots.at[me],
+            send_sem=rs_send.at[j], recv_sem=rs_recv.at[me],
+            device_id=device(j * step), device_id_type=MESH,
+        )
+
+    def start_scatter(j, carry):
+        pl.when(j * step != me)(lambda: scatter(j).start())
+        return carry
+
+    def end_scatter(j, carry):
+        pl.when(j * step != me)(lambda: scatter(j).wait_send())
+        return carry
+
+
+    def gather(i):
+        to = lax.rem(me + i, devices)
+        return pltpu.make_async_remote_copy(
+            src_ref=red, dst_ref=total.at[pl.ds(8 * mine, 8)],
+            send_sem=ag_send.at[i], recv_sem=ag_recv.at[mine],
+            device_id=device(to), device_id_type=MESH,
+        )
+
+
+    lax.fori_loop(0, owners - 1, start_scatter, 0)
     arrive(f, 0)
     arrive(k, 1)
     tiles = size_y // 8
@@ -165,8 +211,30 @@
     stencil(f, k, v, middle)
     exchange(v, 2, (0, 1))
 
-    loads[2].wait()
-    cells = hist.shape[0] // past
+    @pl.when(is_owner)
+    def _():
+        own = pl.ds(pl.multiple_of(8 * mine, 8), 8)
+        slots[me] = gram[own, :]
+
+        def take(i, carry):
+            source = lax.rem(me + i, devices)
+            pltpu.make_async_remote_copy(
+                src_ref=gram.at[pl.ds(0, 8)], dst_ref=slots.at[source],
+                send_sem=rs_send.at[0], recv_sem=rs_recv.at[source],
+                device_id=device(source), device_id_type=MESH,
+            ).wait_recv()
+            return carry
+
+        lax.fori_loop(1, devices, take, 0)
+        red[...] = jnp.sum(slots[...], axis=0) * (1.0 / (cells * samples * devices))
+        total[own, :] = red[...]
+
+        def give(i, carry):
+            gather(i).start()
+            return carry
+
+        lax.fori_loop(1, devices, give, 0)
+
     block[pl.ds(past * cells, cells), :] = sample(v, pick, size_y // 4)
     sent(f, 0)
     sent(k, 1)
@@ -177,72 +245,48 @@
     block[pl.ds((past + 1) * cells, cells), :] = sample(f, pick, size_y // 4)
     sent(v, 2)
 
-    def pair(p, acc):
+    def tail(p, acc):
         x = jnp.concatenate(
-            [block[pl.ds(2 * p, snaps, stride=cells), :], block[pl.ds(2 * p + 1, snaps, stride=cells), :]], axis=1
-        )
-        both = jnp.concatenate(split(x), axis=0)
-        s[p] = both
-        return acc + dot(both, both, (1, 1))
-
-    acc = lax.fori_loop(0, cells // 2, pair, jnp.zeros((2 * snaps, 2 * snaps), F32))
-    gram[...] = (acc[:snaps, :snaps] + acc[snaps:, snaps:]) + (acc[:snaps, snaps:] + acc[snaps:, :snaps])
+            [
+                block[pl.ds((snaps - 16) * cells + 2 * p, 16, stride=cells), :],
+                block[pl.ds((snaps - 16) * cells + 2 * p + 1, 16, stride=cells), :],
+            ],
+            axis=1,
+        )
+        hi, low = split(x)
+        s[p, pl.ds(snaps - 16, 16), :] = hi
+        s[p, pl.ds(2 * snaps - 16, 16), :] = low
+        return acc + dot(jnp.concatenate([hi, low], axis=0), s[p], (1, 1))
+
+    acc = lax.fori_loop(0, cells // 2, tail, jnp.zeros((32, 2 * snaps), F32), unroll=4)
+    acc = acc[8:16] + acc[24:]
+    ends[me] = acc[:, :snaps] + acc[:, snaps:]
     keep = pltpu.make_async_copy(s, s_o, load.at[1])
     keep.start()
 
-    is_owner = lax.rem(me, step) == 0
-    mine = lax.div(me, step)
-
-    def scatter(j):
+    def swap(i, source):
         return pltpu.make_async_remote_copy(
-            src_ref=gram.at[pl.ds(8 * j, 8)], dst_ref=slots.at[me],
-            send_sem=rs_send.at[j], recv_sem=rs_recv.at[me],
-            device_id=device(j * step), device_id_type=MESH,
-        )
-
-    def start_scatter(j, carry):
-        pl.when(j * step != me)(lambda: scatter(j).start())
-        return carry
-
-    def end_scatter(j, carry):
-        pl.when(j * step != me)(lambda: scatter(j).wait_send())
-        return carry
-
-    lax.fori_loop(0, owners, start_scatter, 0)
-
-    def gather(i):
-        to = lax.rem(me + i, devices)
-        return pltpu.make_async_remote_copy(
-            src_ref=red, dst_ref=total.at[pl.ds(8 * mine, 8)],
-            send_sem=ag_send.at[i], recv_sem=ag_recv.at[mine],
-            device_id=device(to), device_id_type=MESH,
-        )
-
+            src_ref=ends.at[me], dst_ref=ends.at[source],
+            send_sem=end_send.at[i], recv_sem=end_recv.at[source],
+            device_id=device(lax.rem(me + i, devices)), device_id_type=MESH,
+        )
+
+    def start_swap(i, carry):
+        swap(i, me).start()
+        return carry
+
+    def end_swap(i, carry):
+        swap(i, lax.rem(me + i, devices)).wait_recv()
+        return carry
+
+    def sent_swap(i, carry):
+        swap(i, me).wait_send()
+        return carry
+
+    lax.fori_loop(1, devices, start_swap, 0)
 
     @pl.when(is_owner)
     def _():
-        own = pl.ds(pl.multiple_of(8 * mine, 8), 8)
-        slots[me] = gram[own, :]
-
-        def take(i, carry):
-            source = lax.rem(me + i, devices)
-            pltpu.make_async_remote_copy(
-                src_ref=gram.at[pl.ds(0, 8)], dst_ref=slots.at[source],
-                send_sem=rs_send.at[0], recv_sem=rs_recv.at[source],
-                device_id=device(source), device_id_type=MESH,
-            ).wait_recv()
-            return carry
-
-        lax.fori_loop(1, devices, take, 0)
-        red[...] = jnp.sum(slots[...], axis=0) * (1.0 / (cells * samples * devices))
-        total[own, :] = red[...]
-
-        def give(i, carry):
-            gather(i).start()
-            return carry
-
-        lax.fori_loop(1, devices, give, 0)
-
         def given(i, carry):
             gather(i).wait_send()
             return carry
@@ -260,8 +304,11 @@
 
         return carry
 
-    lax.fori_loop(0, owners, get, 0)
-    lax.fori_loop(0, owners, end_scatter, 0)
+    lax.fori_loop(0, owners - 1, get, 0)
+    lax.fori_loop(0, owners - 1, end_scatter, 0)
+    lax.fori_loop(1, devices, end_swap, 0)
+    total[pl.ds(snaps - 8, 8), :] = jnp.sum(ends[...], axis=0) * (1.0 / (cells * samples * devices))
+    lax.fori_loop(1, devices, sent_swap, 0)
     gram_o[...] = total[...]
     out.wait()
     keep.wait()
@@ -305,7 +352,9 @@
     keep.start()
     get = pltpu.make_async_copy(s, s_v, sem.at[1])
     get.start()
-    factor, inverse = eliminate(gram[...])
+    row = lax.broadcasted_iota(jnp.int32, (snaps, snaps), 0)
+    col = lax.broadcasted_iota(jnp.int32, (snaps, snaps), 1)
+    factor, inverse = eliminate(jnp.where(col <= row, gram[...], gram[...].T))
     factor_o[...] = factor
     hi, low = split(inverse)
     both = jnp.concatenate([jnp.concatenate([hi, hi], axis=1), jnp.concatenate([low, low], axis=1)], axis=0)
@@ -361,8 +410,10 @@
             pltpu.VMEM((devices, 8, snaps), F32),
             pltpu.VMEM((8, snaps), F32),
             pltpu.VMEM((snaps, snaps), F32),
+            pltpu.VMEM((devices, 8, snaps), F32),
             dma((3,)), dma((3, 4)), dma((3, 4)),
             dma((owners,)), dma((devices,)), dma((devices,)), dma((owners,)),
+            dma((devices,)), dma((devices,)),
         ],
         compiler_params=pltpu.CompilerParams(
             collective_id=0, has_side_effects=True, vmem_limit_bytes=48 << 20

time: 73.5 us -> 50.9 us (0.69)
  Pallas kernels: 72.8 us -> 50.1 us
    pallas_call x1, Pallas kernels: 64.2 us -> 41.4 us  [body(): pl.pallas_call(functools.partial(evolve, nx, ny, past), out_shape=[jax.Sh...]
where the time goes in v2:
time: 50.9 us; the launch traced here: 50.7 us
  Pallas kernels  50.1 us (98%)
  between operations  0.64 us (1%)
    pallas_call x1, Pallas kernels, body(): pl.pallas_call(functools.partial(evolve, nx, ny, past), out_shape=[jax.Sh...  41.4 us
    pallas_call x1, Pallas kernels, body(): pl.pallas_call(orthogonalize, out_shape=[jax.ShapeDtypeStruct((snaps, sna...  8.63 us

profile of v2, /device:TPU:0, one launch (start us, length us, event | category | flops | bytes accessed | tf_op | source)
XLA Modules:
  0.0 50.7 jit_solution(2006635979004211929)
XLA Ops:
  0.6 41.4 %evolve.1 = (f32[16,32,1536]{2,1,0:T(8,128)S(1)}, bf16[32,256,256]{2,1,0:T(8,128)(2,1)}, f32[128,128]{1,0:T(8,128)S(1)}) custom-call(f32[16,32,1536]{2,1,0:T(8,128)} %field.1, f32[16,32,1536]{2,1,0:T(8,128)} %kappa.1, f32[8064,128]{1,0:T(8,128)} %bitcast.1), custom_call_target="tpu_custom_call" | custom-call | tf_op jit(solution)/shard_map/evolve/pallas_call | solution.py:396
  42.1 8.6 %orthogonalize.1 = (f32[128,128]{1,0:T(8,128)}, f32[128,8,8,128]{3,2,1,0:T(8,128)}, f32[16,32,1536]{2,1,0:T(8,128)}) custom-call(f32[128,128]{1,0:T(8,128)S(1)} %get-tuple-element.9.gram, bf16[32,256,256]{2,1,0:T(8,128)(2,1)} %get-tuple-element.10.s, f32[16,32,1536]{2,1,0:T(8,128)S(1)} %get-tuple-element.11.second), custom_call_target="tpu_custom_call" | custom-call | tf_op jit(solution)/shard_map/orthogonalize/pallas_call | solution.py:423

commit v3 on v2

--- a/solution.py
+++ b/solution.py
@@ -24,8 +24,8 @@
     return hi, (x - hi.astype(F32)).astype(BF16)
 
 
-def stencil(v, k, out, tiles):
-    size_x = v.shape[0] - 2
+def stencil(v, k, out, tiles, start, stop):
+    unroll = next(u for u in (8, 7, 4, 2, 1) if (stop - start) % u == 0)
     depth = v.shape[2]
     lane = lax.broadcasted_iota(jnp.int32, (8, depth), 1)
 
@@ -51,8 +51,8 @@
             out[x, rows, :] = c + 0.5 * acc
             return ahead
 
-        first = (k[0, rows, :] + k[1, rows, :]) * (v[1, rows, :] - v[0, rows, :])
-        lax.fori_loop(1, size_x + 1, layer, first, unroll=4)
+        first = (k[start - 1, rows, :] + k[start, rows, :]) * (v[start, rows, :] - v[start - 1, rows, :])
+        lax.fori_loop(start, stop, layer, first, unroll=unroll)
 
 
 def sample(v, pick, rows_y):
@@ -161,15 +161,24 @@
     cells = hist.shape[0] // past
     block[pl.ds(past * cells, 2 * cells), :] = jnp.zeros((2 * cells, samples), F32)
 
-    def pair(p, acc):
-        x = jnp.concatenate(
-            [block[pl.ds(2 * p, snaps, stride=cells), :], block[pl.ds(2 * p + 1, snaps, stride=cells), :]], axis=1
-        )
-        both = jnp.concatenate(split(x), axis=0)
-        s[p] = both
+    def group(first, rows, start):
+        wide = []
+        for p in range(4):
+            at = start * cells + 8 * first + 2 * p
+            x = jnp.concatenate(
+                [block[pl.ds(at, rows, stride=cells), :], block[pl.ds(at + 1, rows, stride=cells), :]], axis=1
+            )
+            hi, low = split(x)
+            s[4 * first + p, pl.ds(start, rows), :] = hi
+            s[4 * first + p, pl.ds(snaps + start, rows), :] = low
+            wide.append(jnp.concatenate([hi, low], axis=0))
+        return jnp.concatenate(wide, axis=1)
+
+    def pair(q, acc):
+        both = group(q, snaps, 0)
         return acc + dot(both, both, (1, 1))
 
-    acc = lax.fori_loop(0, cells // 2, pair, jnp.zeros((2 * snaps, 2 * snaps), F32), unroll=2)
+    acc = lax.fori_loop(0, cells // 8, pair, jnp.zeros((2 * snaps, 2 * snaps), F32))
     gram[...] = (acc[:snaps, :snaps] + acc[snaps:, snaps:]) + (acc[:snaps, snaps:] + acc[snaps:, :snaps])
 
     is_owner = (lax.rem(me, step) == 0) & (me < (owners - 1) * step)
@@ -206,9 +215,9 @@
     tiles = size_y // 8
     edge = sorted({0, tiles - 1})
     middle = [t for t in range(tiles) if t not in edge]
-    stencil(f, k, v, edge)
+    stencil(f, k, v, edge, 1, size_x + 1)
     exchange(v, 2, (2, 3))
-    stencil(f, k, v, middle)
+    stencil(f, k, v, middle, 1, size_x + 1)
     exchange(v, 2, (0, 1))
 
     @pl.when(is_owner)
@@ -238,27 +247,22 @@
     block[pl.ds(past * cells, cells), :] = sample(v, pick, size_y // 4)
     sent(f, 0)
     sent(k, 1)
+    stencil(v, k, f, middle, 2, size_x)
     arrive(v, 2)
-    stencil(v, k, f, range(tiles))
+    stencil(v, k, f, edge, 1, size_x + 1)
+    stencil(v, k, f, middle, 1, 2)
+    stencil(v, k, f, middle, size_x, size_x + 1)
     out = pltpu.make_async_copy(f.at[inner], second_o, load.at[0])
     out.start()
     block[pl.ds((past + 1) * cells, cells), :] = sample(f, pick, size_y // 4)
     sent(v, 2)
 
-    def tail(p, acc):
-        x = jnp.concatenate(
-            [
-                block[pl.ds((snaps - 16) * cells + 2 * p, 16, stride=cells), :],
-                block[pl.ds((snaps - 16) * cells + 2 * p + 1, 16, stride=cells), :],
-            ],
-            axis=1,
-        )
-        hi, low = split(x)
-        s[p, pl.ds(snaps - 16, 16), :] = hi
-        s[p, pl.ds(2 * snaps - 16, 16), :] = low
-        return acc + dot(jnp.concatenate([hi, low], axis=0), s[p], (1, 1))
-
-    acc = lax.fori_loop(0, cells // 2, tail, jnp.zeros((32, 2 * snaps), F32), unroll=4)
+    def tail(q, acc):
+        both = group(q, 16, snaps - 16)
+        all_rows = jnp.concatenate([s[4 * q + p] for p in range(4)], axis=1)
+        return acc + dot(both, all_rows, (1, 1))
+
+    acc = lax.fori_loop(0, cells // 8, tail, jnp.zeros((32, 2 * snaps), F32))
     acc = acc[8:16] + acc[24:]
     ends[me] = acc[:, :snaps] + acc[:, snaps:]
     keep = pltpu.make_async_copy(s, s_o, load.at[1])

time: 50.9 us -> 48.2 us (0.947)
  Pallas kernels: 50.1 us -> 47.4 us
    pallas_call x1, Pallas kernels: 41.4 us -> 38.7 us  [body(): pl.pallas_call(functools.partial(evolve, nx, ny, past), out_shape=[jax.Sh...]
where the time goes in v3:
time: 48.2 us; the launch traced here: 48 us
  Pallas kernels  47.4 us (98%)
  between operations  0.64 us (1%)
    pallas_call x1, Pallas kernels, body(): pl.pallas_call(functools.partial(evolve, nx, ny, past), out_shape=[jax.Sh...  38.7 us
    pallas_call x1, Pallas kernels, body(): pl.pallas_call(orthogonalize, out_shape=[jax.ShapeDtypeStruct((snaps, sna...  8.63 us

profile of v3, /device:TPU:0, one launch (start us, length us, event | category | flops | bytes accessed | tf_op | source)
XLA Modules:
  0.0 48.0 jit_solution(11356324188100123259)
XLA Ops:
  0.6 38.7 %evolve.1 = (f32[16,32,1536]{2,1,0:T(8,128)S(1)}, bf16[32,256,256]{2,1,0:T(8,128)(2,1)}, f32[128,128]{1,0:T(8,128)S(1)}) custom-call(f32[16,32,1536]{2,1,0:T(8,128)} %field.1, f32[16,32,1536]{2,1,0:T(8,128)} %kappa.1, f32[8064,128]{1,0:T(8,128)} %bitcast.1), custom_call_target="tpu_custom_call" | custom-call | tf_op jit(solution)/shard_map/evolve/pallas_call | solution.py:400
  39.4 8.6 %orthogonalize.1 = (f32[128,128]{1,0:T(8,128)}, f32[128,8,8,128]{3,2,1,0:T(8,128)}, f32[16,32,1536]{2,1,0:T(8,128)}) custom-call(f32[128,128]{1,0:T(8,128)S(1)} %get-tuple-element.9.gram, bf16[32,256,256]{2,1,0:T(8,128)(2,1)} %get-tuple-element.10.s, f32[16,32,1536]{2,1,0:T(8,128)S(1)} %get-tuple-element.11.second), custom_call_target="tpu_custom_call" | custom-call | tf_op jit(solution)/shard_map/orthogonalize/pallas_call | solution.py:427
